TPU v7x, 32 devices: a whole 2x2x4 slice. The times are simulated.
32 devices in a mesh: freq: 4 (over y, x), cell: 8 (over z, core).
Axes of the slice: x: 2, y: 2, z: 4, core: 2. Of those that a mesh axis runs over, the one named last changes fastest.
Arguments:
- snapshots: bfloat16 [8, 2, 16, 512], P('freq', None, 'cell'), may hold values from -6 to 6
- previous: float32 [8, 2, 512, 512], P('freq', None, 'cell'), may hold values from -40 to 40, as said below
- replicas: bfloat16 [8, 2, 8192, 512], P('freq', None, 'cell'), may hold values from -1 to 1, as said below
Outputs:
- power: float32 [8192], P('cell')
- csdm: float32 [8, 2, 512, 512], P('freq', None, 'cell')
Inputs may be any that keep to these rules, and one draw needn't show every extreme that they name: `previous`: for every frequency the real part is symmetric with a positive diagonal and the imaginary part is antisymmetric. `replicas`: every entry of a replica vector has modulus 1 / sqrt(512) up to bfloat16 rounding.
All inputs are finite; a program needn't handle non-finite values.
Results may differ from a plain program's by a relative error of at most 0.0003.
Values may be sent and summed in bfloat16 or wider, within the bound.
A program may use at most 64 MiB of HBM per device.

v0:
```python
import functools

import jax
import jax.numpy as jnp
from jax import lax
from jax.experimental import pallas as pl
from jax.experimental.pallas import tpu as pltpu
from jax.sharding import PartitionSpec as P

LINK = jnp.bfloat16
LIFT = 2.0**15.5
MESH = pl.DeviceIdType.MESH


def encode(x):
    x2 = x * x
    x4 = x2 * x2
    x8 = x4 * x4
    return jnp.where(x < 0, -x8, x8).astype(LINK)


def decode(y):
    y = y.astype(jnp.float32)
    root = jnp.exp(0.125 * jnp.log(jnp.maximum(jnp.abs(y), 1e-37)))
    return jnp.where(y < 0, -root, root)


def contract_rows(a, b):
    return lax.dot_general(
        a, b, (((0,), (0,)), ((), ())), preferred_element_type=jnp.float32
    )


def dot(a, b):
    return jnp.dot(a, b, preferred_element_type=jnp.float32)


def kernel(
    n, nf, snap_ref, prev_ref, rep_hbm, power_ref, csdm_ref,
    hbuf, mbuf, rep, cross_re, cross_im, high, low, lanes, slots,
    hsend, hrecv, fsend, frecv, msend, mrecv, gsend, grecv, psend, precv, rsem,
):
    F, _, S, M = snap_ref.shape
    R = prev_ref.shape[2]
    T = mbuf.shape[1]
    cells = rep.shape[2]
    chips = n // 2
    me = lax.axis_index("cell")
    fr = lax.axis_index("freq")
    chip, core = me // 2, lax.rem(me, 2)
    sib = chip * 2 + 1 - core

    loads = [pltpu.make_async_copy(rep_hbm.at[f], rep.at[f], rsem.at[f]) for f in range(F)]
    for f in range(F):
        loads[f].start()

    def ahead(d):
        return lax.rem(chip + d, chips) * 2 + core

    def behind(d):
        return lax.rem(chip + chips - d, chips) * 2 + core

    barrier = pltpu.get_barrier_semaphore()
    for d in range(1, chips):
        pl.semaphore_signal(barrier, inc=1, device_id=(fr, ahead(d)), device_id_type=MESH)
    pl.semaphore_signal(barrier, inc=1, device_id=(fr, sib), device_id_type=MESH)
    for d in range(1, nf):
        pl.semaphore_signal(barrier, inc=1, device_id=(lax.rem(fr + d, nf), me), device_id_type=MESH)

    row = lax.broadcasted_iota(jnp.int32, (T, M), 0)
    message = jnp.zeros((T, M), jnp.float32)
    for f in range(F):
        for p in range(2):
            values = snap_ref[f, p].astype(jnp.float32)
            for s in range(S):
                message = jnp.where(row == (f * 2 + p) * S + s, values[s : s + 1, :], message)
        h = prev_ref[f, 0] + prev_ref[f, 1]
        top = jnp.max(jnp.max(jnp.abs(h), axis=1, keepdims=True), axis=0, keepdims=True)
        scale = jnp.maximum(top, 1e-30).astype(jnp.bfloat16).astype(jnp.float32)
        hbuf[me, f] = encode(h * (LIFT / scale))
        message = jnp.where(row == 2 * S * F + f, scale, message)
    mbuf[me] = message.astype(jnp.bfloat16)

    def remote(ref, send, recv, to):
        return pltpu.make_async_remote_copy(
            src_ref=ref, dst_ref=ref, send_sem=send, recv_sem=recv,
            device_id=(fr, to), device_id_type=MESH,
        )

    pl.semaphore_wait(barrier, chips - 1 + 1 + nf - 1)

    sends = []
    for d in range(chips - 1, 0, -1):
        c = remote(mbuf.at[me], msend.at[d], mrecv.at[d], ahead(d))
        c.start()
        sends.append(c)
    c = remote(mbuf.at[me], msend.at[0], mrecv.at[0], sib)
    c.start()
    sends.append(c)
    for f in range(F):
        for d in range(chips - 1, 0, -1):
            c = remote(hbuf.at[me, f], hsend.at[f, d], hrecv.at[f, d], ahead(d))
            c.start()
            sends.append(c)
        c = remote(hbuf.at[me, f], hsend.at[f, 0], hrecv.at[f, 0], sib)
        c.start()
        sends.append(c)

    def other(d):
        return lax.rem(chip + chips - d, chips) * 2 + 1 - core

    for d in range(1, chips):
        ref = mbuf.at[behind(d)]
        remote(ref, msend.at[d], mrecv.at[d], sib).wait_recv()
        c = remote(ref, gsend.at[d], grecv.at[d], sib)
        c.start()
        sends.append(c)
    remote(mbuf.at[sib], msend.at[0], mrecv.at[0], sib).wait_recv()
    for d in range(1, chips):
        remote(mbuf.at[other(d)], gsend.at[d], grecv.at[d], sib).wait_recv()

    factor = 0.2 / (S * n)
    G = mbuf[...].reshape(n * T, M)
    a = lax.broadcasted_iota(jnp.int32, (n * T, n * T), 0)
    b = lax.broadcasted_iota(jnp.int32, (n * T, n * T), 1)
    place = lax.rem(a, T)
    used = place < 2 * S * F
    imag = lax.rem(place, 2 * S) >= S
    turn = jnp.where(used & imag & (b == a - S), 1.0, 0.0) - jnp.where(
        used & jnp.logical_not(imag) & (b == a + S), 1.0, 0.0
    )
    Z = dot(turn.astype(jnp.bfloat16), G).astype(jnp.bfloat16)
    spot = lax.rem(lax.broadcasted_iota(jnp.int32, (n * T, M), 0), T)
    Gf = G.astype(jnp.float32)
    mine = pl.ds(pl.multiple_of(me * R, R), R)
    for f in range(F):
        inside = (spot >= 2 * S * f) & (spot < 2 * S * (f + 1))
        X = jnp.where(inside, Gf, 0.0).astype(jnp.bfloat16)
        cross_re[f] = contract_rows(X, G) * factor
        cross_im[f] = contract_rows(X, Z) * factor
        csdm_ref[f, 0] = 0.8 * prev_ref[f, 0] + cross_re[f, mine]
        csdm_ref[f, 1] = 0.8 * prev_ref[f, 1] + cross_im[f, mine]

    step = min(512, cells)
    for f in range(F):
        for d in range(1, chips):
            ref = hbuf.at[behind(d), f]
            remote(ref, hsend.at[f, d], hrecv.at[f, d], sib).wait_recv()
            c = remote(ref, fsend.at[f, d], frecv.at[f, d], sib)
            c.start()
            sends.append(c)
    for f in range(F):
        remote(hbuf.at[sib, f], hsend.at[f, 0], hrecv.at[f, 0], sib).wait_recv()
        for d in range(1, chips):
            remote(hbuf.at[other(d), f], fsend.at[f, d], frecv.at[f, d], sib).wait_recv()
        trace = jnp.zeros((R, M), jnp.float32)
        ii = lax.broadcasted_iota(jnp.int32, (R, M), 0)
        jj = lax.broadcasted_iota(jnp.int32, (R, M), 1)
        for j in range(n):
            at = j * T + 2 * S * F + f
            back = Gf[at : at + 1, :] * (0.8 / LIFT)
            rows = slice(j * R, (j + 1) * R)
            full = decode(hbuf[j, f]) * back + (cross_re[f, rows] + cross_im[f, rows])
            trace = trace + jnp.where(jj == ii + j * R, full, 0.0)
            top = full.astype(jnp.bfloat16)
            high[rows, :] = top
            low[rows, :] = (full - top.astype(jnp.float32)).astype(jnp.bfloat16)
        total = jnp.sum(jnp.sum(trace, axis=0, keepdims=True), axis=1, keepdims=True)
        gain = (M / (F * nf)) / total
        loads[f].wait()
        for t in range(cells // step):
            at = slice(t * step, (t + 1) * step)
            u, v = rep[f, 0, at], rep[f, 1, at]
            yu = dot(u, high[...]) + dot(u, low[...])
            yv = dot(v, high[...]) + dot(v, low[...])
            uf, vf = u.astype(jnp.float32), v.astype(jnp.float32)
            terms = yu * (uf - vf) + yv * (uf + vf)
            part = terms[:, 0:128]
            for k in range(1, M // 128):
                part = part + terms[:, k * 128 : (k + 1) * 128]
            part = part * gain
            lanes[at] = part if f == 0 else lanes[at] + part

    slots[fr] = jnp.sum(lanes[...].T, axis=0, keepdims=True)
    for d in range(1, nf):
        c = pltpu.make_async_remote_copy(
            src_ref=slots.at[fr], dst_ref=slots.at[fr], send_sem=psend.at[d], recv_sem=precv.at[d],
            device_id=(lax.rem(fr + d, nf), me), device_id_type=MESH,
        )
        c.start()
        sends.append(c)
    for d in range(1, nf):
        ref = slots.at[lax.rem(fr + nf - d, nf)]
        pltpu.make_async_remote_copy(
            src_ref=ref, dst_ref=ref, send_sem=psend.at[d], recv_sem=precv.at[d],
            device_id=(lax.rem(fr + d, nf), me), device_id_type=MESH,
        ).wait_recv()
    power = slots[0]
    for k in range(1, nf):
        power = power + slots[k]
    power_ref[...] = power
    for c in sends:
        c.wait_send()


def on_device(snapshots, previous, replicas):
    F, _, R, M = previous.shape
    S = snapshots.shape[2]
    cells = replicas.shape[2]
    n, nf = lax.axis_size("cell"), lax.axis_size("freq")
    chips = n // 2
    T = -(-(2 * S * F + F) // 16) * 16
    dma = pltpu.SemaphoreType.DMA
    vmem = pl.BlockSpec(memory_space=pltpu.VMEM)
    power, csdm = pl.pallas_call(
        functools.partial(kernel, n, nf),
        out_shape=(
            jax.ShapeDtypeStruct((1, cells), jnp.float32),
            jax.ShapeDtypeStruct(previous.shape, jnp.float32),
        ),
        in_specs=[vmem, vmem, pl.BlockSpec(memory_space=pl.ANY)],
        out_specs=(vmem, vmem),
        scratch_shapes=[
            pltpu.VMEM((n, F, R, M), LINK),
            pltpu.VMEM((n, T, M), jnp.bfloat16),
            pltpu.VMEM(replicas.shape, jnp.bfloat16),
            pltpu.VMEM((F, M, M), jnp.float32),
            pltpu.VMEM((F, M, M), jnp.float32),
            pltpu.VMEM((M, M), jnp.bfloat16),
            pltpu.VMEM((M, M), jnp.bfloat16),
            pltpu.VMEM((cells, 128), jnp.float32),
            pltpu.VMEM((nf, 1, cells), jnp.float32),
            dma((F, chips)), dma((F, chips)), dma((F, chips)), dma((F, chips)),
            dma((chips,)), dma((chips,)), dma((chips,)), dma((chips,)),
            dma((nf,)), dma((nf,)), dma((F,)),
        ],
        compiler_params=pltpu.CompilerParams(
            collective_id=0, has_side_effects=True, vmem_limit_bytes=48 * 1024 * 1024
        ),
    )(snapshots, previous, replicas)
    return (power.reshape(cells), csdm)


def solution(mesh):
    placed = (
        P("freq", None, "cell", None),
        P("freq", None, "cell", None),
        P("freq", None, "cell", None),
    )
    return jax.shard_map(
        on_device,
        mesh=mesh,
        in_specs=placed,
        out_specs=(P("cell"), P("freq", None, "cell", None)),
        check_vma=False,
    )
```

profile of v0, /device:TPU:0, one launch (start us, length us, event | category | flops | bytes accessed | tf_op | source)
XLA Modules:
  0.0 36.3 jit_solution(12452630422993416058)
XLA Ops:
  0.6 0.0 copy-start
  0.6 2.2 %copy-done = bf16[2,2,1024,512]{3,2,1,0:T(8,128)(2,1)S(1)} copy-done((bf16[2,2,1024,512]{3,2,1,0:T(8,128)(2,1)S(1)}, bf16[2,2,1024,512]{3,2,1,0:T(8,128)(2,1)}, u32[]{:S(2)}) %copy-start) | copy-done | bytes 4194328
  2.8 0.0 copy-start.1
  2.8 1.0 %copy-done.1 = f32[2,2,64,512]{3,2,1,0:T(8,128)S(1)} copy-done((f32[2,2,64,512]{3,2,1,0:T(8,128)S(1)}, f32[2,2,64,512]{3,2,1,0:T(8,128)}, u32[]{:S(2)}) %copy-start.1) | copy-done | bytes 524312
  3.9 0.0 copy-start.2
  3.9 0.7 %copy-done.2 = bf16[2,2,2,512]{3,2,1,0:T(2,128)(2,1)S(1)} copy-done((bf16[2,2,2,512]{3,2,1,0:T(2,128)(2,1)S(1)}, bf16[2,2,2,512]{3,2,1,0:T(2,128)(2,1)}, u32[]{:S(2)}) %copy-start.2) | copy-done | bytes 8216
  4.6 30.3 %shard_map.50 = (f32[1,1024]{1,0:T(1,128)S(1)}, f32[2,2,64,512]{3,2,1,0:T(8,128)S(1)}) custom-call(bf16[2,2,2,512]{3,2,1,0:T(2,128)(2,1)S(1)} %copy-done.2, f32[2,2,64,512]{3,2,1,0:T(8,128)S(1)} %copy-done.1, bf16[2,2,1024,512]{3,2,1,0:T(8,128)(2,1)S(1)} %copy-done), custom_call_target="tpu_custom_call" | custom-call | tf_op jit(solution)/shard_map/pallas_call | solution.py:215
  34.9 0.6 %copy.7 = f32[1024]{0:T(1024)} copy(f32[1024]{0:T(1024)S(1)} %bitcast.1) | data formatting | bytes 8192
  35.5 0.8 %copy.8 = f32[2,2,64,512]{3,2,1,0:T(8,128)} copy(f32[2,2,64,512]{3,2,1,0:T(8,128)S(1)} %get-tuple-element.9) | data formatting | bytes 1048576
Async XLA Ops:
  0.6 2.2 %copy-start = (bf16[2,2,1024,512]{3,2,1,0:T(8,128)(2,1)S(1)}, bf16[2,2,1024,512]{3,2,1,0:T(8,128)(2,1)}, u32[]{:S(2)}) copy-start(bf16[2,2,1024,512]{3,2,1,0:T(8,128)(2,1)} %rep_hbm.1) | copy-start | bytes 12582916
  2.8 1.0 %copy-start.1 = (f32[2,2,64,512]{3,2,1,0:T(8,128)S(1)}, f32[2,2,64,512]{3,2,1,0:T(8,128)}, u32[]{:S(2)}) copy-start(f32[2,2,64,512]{3,2,1,0:T(8,128)} %prev_ref.1) | copy-start | bytes 1572868
  3.9 0.7 %copy-start.2 = (bf16[2,2,2,512]{3,2,1,0:T(2,128)(2,1)S(1)}, bf16[2,2,2,512]{3,2,1,0:T(2,128)(2,1)}, u32[]{:S(2)}) copy-start(bf16[2,2,2,512]{3,2,1,0:T(2,128)(2,1)} %snap_ref.1) | copy-start | bytes 24580
where the time goes:
time: 36.5 us; the launch traced here: 36.3 us
  Pallas kernels  30.3 us (83%)
  local copies, waits for them, and re-layouts  5.31 us (15%)
  between operations  0.65 us (2%)
    pallas_call x1, Pallas kernels, on_device(): pl.pallas_call(functools.partial(kernel, n, nf), out_shape=(jax.ShapeDtyp...  30.3 us
    unnamed x8, local copies, waits for them, and re-layouts  5.31 us

commit v1 on v0

v1 whole, which is shorter than its diff:
```python
import functools

import jax
import jax.numpy as jnp
from jax import lax
from jax.experimental import pallas as pl
from jax.experimental.pallas import tpu as pltpu
from jax.sharding import PartitionSpec as P

LINK = jnp.bfloat16
LIFT = 2.0**15.5
MESH = pl.DeviceIdType.MESH


def encode(x):
    x2 = x * x
    x4 = x2 * x2
    x8 = x4 * x4
    return jnp.where(x < 0, -x8, x8).astype(LINK)


def decode(y):
    y = y.astype(jnp.float32)
    root = jnp.exp(0.125 * jnp.log(jnp.maximum(jnp.abs(y), 1e-37)))
    return jnp.where(y < 0, -root, root)


def contract_rows(a, b):
    return lax.dot_general(
        a, b, (((0,), (0,)), ((), ())), preferred_element_type=jnp.float32
    )


def dot(a, b):
    return jnp.dot(a, b, preferred_element_type=jnp.float32)


def kernel(
    n, nf, snap_ref, prev_hbm, rep_hbm, power_ref, csdm_ref,
    hbuf, mbuf, prev_ref, rep, cross_re, cross_im, weights, diag, lanes, slots,
    osend, zrecv, zsend, srecv, ssend, msend, mrecv, gsend, grecv, psend, precv, rsem, vsem,
):
    F, _, S, M = snap_ref.shape
    R = prev_ref.shape[2]
    T = mbuf.shape[1]
    cells = rep.shape[2]
    chips = n // 2
    group = 128
    per = group // R
    me = lax.axis_index("cell")
    fr = lax.axis_index("freq")
    chip, core = me // 2, lax.rem(me, 2)
    sib = chip * 2 + 1 - core

    barrier = pltpu.get_barrier_semaphore()
    for d in range(1, chips):
        pl.semaphore_signal(
            barrier, inc=1, device_id=(fr, lax.rem(chip + d, chips) * 2 + core), device_id_type=MESH
        )
    pl.semaphore_signal(barrier, inc=1, device_id=(fr, sib), device_id_type=MESH)
    for d in range(1, nf):
        pl.semaphore_signal(barrier, inc=1, device_id=(lax.rem(fr + d, nf), me), device_id_type=MESH)

    earlier = pltpu.make_async_copy(prev_hbm, prev_ref, vsem)
    earlier.start()
    loads = [pltpu.make_async_copy(rep_hbm.at[f], rep.at[f], rsem.at[f]) for f in range(F)]
    for f in range(F):
        loads[f].start()

    def ahead(d):
        return lax.rem(chip + d, chips) * 2 + core

    def behind(d):
        return lax.rem(chip + chips - d, chips) * 2 + core

    def other(d):
        return lax.rem(chip + chips - d, chips) * 2 + 1 - core

    def remote(ref, send, recv, to):
        return pltpu.make_async_remote_copy(
            src_ref=ref, dst_ref=ref, send_sem=send, recv_sem=recv,
            device_id=(fr, to), device_id_type=MESH,
        )

    earlier.wait()
    row = lax.broadcasted_iota(jnp.int32, (T, M), 0)
    message = jnp.zeros((T, M), jnp.float32)
    for f in range(F):
        for p in range(2):
            values = snap_ref[f, p].astype(jnp.float32)
            for s in range(S):
                message = jnp.where(row == (f * 2 + p) * S + s, values[s : s + 1, :], message)
        h = prev_ref[f, 0] + prev_ref[f, 1]
        top = jnp.max(jnp.max(jnp.abs(h), axis=1, keepdims=True), axis=0, keepdims=True)
        scale = jnp.maximum(top, 1e-30).astype(jnp.bfloat16).astype(jnp.float32)
        hbuf[me, f] = encode(h * (LIFT / scale))
        message = jnp.where(row == 2 * S * F + f, scale, message)
    mbuf[me] = message.astype(jnp.bfloat16)

    pl.semaphore_wait(barrier, chips - 1 + 1 + nf - 1)

    sends = []
    for d in range(chips - 1, 0, -1):
        c = remote(mbuf.at[me], msend.at[d], mrecv.at[d], ahead(d))
        c.start()
        sends.append(c)
    c = remote(mbuf.at[me], msend.at[0], mrecv.at[0], sib)
    c.start()
    sends.append(c)

    has_up, has_down = chip + 1 < chips, chip > 0
    up_to, down_to = lax.rem(me + 2, n), lax.rem(me + n - 2, n)
    for f in range(F):
        own = hbuf.at[me, f]

        @pl.when(has_up)
        def _():
            remote(own, osend.at[f, 0], zrecv.at[f, 0, 1], up_to).start()

        @pl.when(has_down)
        def _():
            remote(own, osend.at[f, 1], zrecv.at[f, 1, 1], down_to).start()

        c = remote(own, osend.at[f, 2], srecv.at[f, 1, 0], sib)
        c.start()
        sends.append(c)

    for f in range(F):
        diag[f] = jnp.zeros((1, M), jnp.float32)
        lanes[f] = jnp.zeros((cells, 128), jnp.float32)

    for d in range(1, chips):
        ref = mbuf.at[behind(d)]
        remote(ref, msend.at[d], mrecv.at[d], sib).wait_recv()
        c = remote(ref, gsend.at[d], grecv.at[d], sib)
        c.start()
        sends.append(c)
    remote(mbuf.at[sib], msend.at[0], mrecv.at[0], sib).wait_recv()
    for d in range(1, chips):
        remote(mbuf.at[other(d)], gsend.at[d], grecv.at[d], sib).wait_recv()

    factor = 0.2 / (S * n)
    G = mbuf[...].reshape(n * T, M)
    a = lax.broadcasted_iota(jnp.int32, (n * T, n * T), 0)
    b = lax.broadcasted_iota(jnp.int32, (n * T, n * T), 1)
    place = lax.rem(a, T)
    used = place < 2 * S * F
    imag = lax.rem(place, 2 * S) >= S
    turn = jnp.where(used & imag & (b == a - S), 1.0, 0.0) - jnp.where(
        used & jnp.logical_not(imag) & (b == a + S), 1.0, 0.0
    )
    Z = dot(turn.astype(jnp.bfloat16), G).astype(jnp.bfloat16)
    spot = lax.rem(lax.broadcasted_iota(jnp.int32, (n * T, M), 0), T)
    Gf = G.astype(jnp.float32)
    mine = pl.ds(pl.multiple_of(me * R, R), R)
    for f in range(F):
        inside = (spot >= 2 * S * f) & (spot < 2 * S * (f + 1))
        X = jnp.where(inside, Gf, 0.0).astype(jnp.bfloat16)
        cross_re[f] = contract_rows(X, G) * factor
        cross_im[f] = contract_rows(X, Z) * factor
        csdm_ref[f, 0] = 0.8 * prev_ref[f, 0] + cross_re[f, mine]
        csdm_ref[f, 1] = 0.8 * prev_ref[f, 1] + cross_im[f, mine]
    for f in range(F):
        loads[f].wait()

    step = min(512, cells)

    def score(g):
        for f in range(F):
            for i in range(per):
                j = g * per + i
                rows = pl.ds(pl.multiple_of(j * R, R), R)
                back = mbuf[j].astype(jnp.float32)[2 * S * F + f : 2 * S * F + f + 1, :] * (0.8 / LIFT)
                full = decode(hbuf[j, f]) * back + (cross_re[f, rows] + cross_im[f, rows])
                ii = lax.broadcasted_iota(jnp.int32, (R, M), 0)
                jj = lax.broadcasted_iota(jnp.int32, (R, M), 1)
                diag[f] += jnp.sum(jnp.where(jj == ii + j * R, full, 0.0), axis=0, keepdims=True)
                top = full.astype(jnp.bfloat16)
                weights[f, i * R : (i + 1) * R] = top
                low = (full - top.astype(jnp.float32)).astype(jnp.bfloat16)
                weights[f, group + i * R : group + (i + 1) * R] = low
            some = pl.ds(pl.multiple_of(g * group, group), group)
            for t in range(cells // step):
                at = slice(t * step, (t + 1) * step)
                us, vs = rep[f, 0, at, some], rep[f, 1, at, some]
                yu = dot(jnp.concatenate([us, us], axis=1), weights[f])
                yv = dot(jnp.concatenate([vs, vs], axis=1), weights[f])
                uf, vf = rep[f, 0, at].astype(jnp.float32), rep[f, 1, at].astype(jnp.float32)
                terms = yu * (uf - vf) + yv * (uf + vf)
                part = terms[:, 0:128]
                for k in range(1, M // 128):
                    part = part + terms[:, k * 128 : (k + 1) * 128]
                lanes[f, at] += part

    below, above = chip, chips - 1 - chip
    both = jnp.minimum(below, above)
    longer = jnp.where(below > above, 1, 0)

    def route(i):
        paired = i <= 2 * both
        k = jnp.where(paired, (i + 1) // 2, i - both)
        up = jnp.where(paired, lax.rem(i, 2), longer)
        return 1 - up, k, chip + k * (1 - 2 * up)

    def onward(f, way, k, q):
        ref = hbuf.at[q * 2 + core, f]
        later = jnp.minimum(k + 1, chips - 1)
        to = jnp.where(way == 0, up_to, down_to)
        return (
            remote(ref, zsend.at[f, way, k], zrecv.at[f, way, later], to),
            remote(ref, ssend.at[f, way, k], srecv.at[f, way, k], sib),
        )

    def goes_on(way):
        return jnp.where(way == 0, jnp.where(has_up, 1, 0), jnp.where(has_down, 1, 0)) == 1

    @pl.loop(0, chips)
    def _(i):
        way, k, q = route(i)
        for f in range(F):
            @pl.when(i > 0)
            def _():
                ref = hbuf.at[q * 2 + core, f]
                remote(ref, zsend.at[f, way, k], zrecv.at[f, way, k], sib).wait_recv()
                further, across = onward(f, way, k, q)

                @pl.when(goes_on(way))
                def _():
                    further.start()

                across.start()
        for f in range(F):
            ref = hbuf.at[q * 2 + 1 - core, f]
            remote(ref, ssend.at[f, way, k], srecv.at[f, way, k], sib).wait_recv()
        if 2 * R == group:
            score(q)

    if 2 * R != group:
        @pl.loop(0, M // group)
        def _(g):
            score(g)

    ready = jnp.zeros((cells, 128), jnp.float32)
    for f in range(F):
        ready = ready + lanes[f] * ((M / (F * nf)) / jnp.sum(diag[f], axis=1, keepdims=True))
    slots[fr] = jnp.sum(ready.T, axis=0, keepdims=True)
    for d in range(1, nf):
        c = pltpu.make_async_remote_copy(
            src_ref=slots.at[fr], dst_ref=slots.at[fr], send_sem=psend.at[d], recv_sem=precv.at[d],
            device_id=(lax.rem(fr + d, nf), me), device_id_type=MESH,
        )
        c.start()
        sends.append(c)

    for f in range(F):
        own = hbuf.at[me, f]

        @pl.when(has_up)
        def _():
            remote(own, osend.at[f, 0], zrecv.at[f, 0, 1], up_to).wait_send()

        @pl.when(has_down)
        def _():
            remote(own, osend.at[f, 1], zrecv.at[f, 1, 1], down_to).wait_send()

    @pl.loop(1, chips)
    def _(i):
        way, k, q = route(i)
        for f in range(F):
            further, across = onward(f, way, k, q)

            @pl.when(goes_on(way))
            def _():
                further.wait_send()

            across.wait_send()

    for d in range(1, nf):
        ref = slots.at[lax.rem(fr + nf - d, nf)]
        pltpu.make_async_remote_copy(
            src_ref=ref, dst_ref=ref, send_sem=psend.at[d], recv_sem=precv.at[d],
            device_id=(lax.rem(fr + d, nf), me), device_id_type=MESH,
        ).wait_recv()
    power = slots[0]
    for k in range(1, nf):
        power = power + slots[k]
    power_ref[...] = power
    for c in sends:
        c.wait_send()


def on_device(snapshots, previous, replicas):
    F, _, R, M = previous.shape
    S = snapshots.shape[2]
    cells = replicas.shape[2]
    n, nf = lax.axis_size("cell"), lax.axis_size("freq")
    chips = n // 2
    T = -(-(2 * S * F + F) // 16) * 16
    dma = pltpu.SemaphoreType.DMA
    vmem = pl.BlockSpec(memory_space=pltpu.VMEM)
    hbm = pl.BlockSpec(memory_space=pltpu.HBM)
    power, csdm = pl.pallas_call(
        functools.partial(kernel, n, nf),
        out_shape=(
            jax.ShapeDtypeStruct((1, cells), jnp.float32),
            jax.ShapeDtypeStruct(previous.shape, jnp.float32),
        ),
        in_specs=[vmem, hbm, hbm],
        out_specs=(vmem, vmem),
        scratch_shapes=[
            pltpu.VMEM((n, F, R, M), LINK),
            pltpu.VMEM((n, T, M), jnp.bfloat16),
            pltpu.VMEM(previous.shape, jnp.float32),
            pltpu.VMEM(replicas.shape, jnp.bfloat16),
            pltpu.VMEM((F, M, M), jnp.float32),
            pltpu.VMEM((F, M, M), jnp.float32),
            pltpu.VMEM((F, 256, M), jnp.bfloat16),
            pltpu.VMEM((F, 1, M), jnp.float32),
            pltpu.VMEM((F, cells, 128), jnp.float32),
            pltpu.VMEM((nf, 1, cells), jnp.float32),
            dma((F, 3)), dma((F, 2, chips)), dma((F, 2, chips)), dma((F, 2, chips)), dma((F, 2, chips)),
            dma((chips,)), dma((chips,)), dma((chips,)), dma((chips,)),
            dma((nf,)), dma((nf,)), dma((F,)), dma,
        ],
        compiler_params=pltpu.CompilerParams(
            collective_id=0, has_side_effects=True, vmem_limit_bytes=64 * 1024 * 1024 - 65536
        ),
    )(snapshots, previous, replicas)
    return (power.reshape(cells), csdm)


def solution(mesh):
    placed = (
        P("freq", None, "cell", None),
        P("freq", None, "cell", None),
        P("freq", None, "cell", None),
    )
    return jax.shard_map(
        on_device,
        mesh=mesh,
        in_specs=placed,
        out_specs=(P("cell"), P("freq", None, "cell", None)),
        check_vma=False,
    )
```

time: 36.5 us -> 37.5 us (1.027)
  Pallas kernels: 30.3 us -> 33.5 us
  local copies, waits for them, and re-layouts: 5.31 us -> 3.13 us
    pallas_call x1, Pallas kernels: 30.3 us -> 33.5 us  [on_device(): pl.pallas_call(functools.partial(kernel, n, nf), out_shape=(jax.ShapeDtyp...]
    unnamed x8 -> x2, local copies, waits for them, and re-layouts: 5.31 us -> 3.13 us
where the time goes in v1:
time: 37.5 us; the launch traced here: 37.3 us
  Pallas kernels  33.5 us (89%)
  local copies, waits for them, and re-layouts  3.13 us (8%)
  between operations  0.64 us (2%)
    pallas_call x1, Pallas kernels, on_device(): pl.pallas_call(functools.partial(kernel, n, nf), out_shape=(jax.ShapeDtyp...  33.5 us
    unnamed x2, local copies, waits for them, and re-layouts  3.13 us

profile of v1, /device:TPU:0, one launch (start us, length us, event | category | flops | bytes accessed | tf_op | source)
XLA Modules:
  0.0 37.3 jit_solution(15454373810457582408)
XLA Ops:
  0.6 33.5 %shard_map.50 = (f32[1,1024]{1,0:T(1,128)}, f32[2,2,64,512]{3,2,1,0:T(8,128)}) custom-call(bf16[2,2,2,512]{3,2,1,0:T(2,128)(2,1)} %snap_ref.1, f32[2,2,64,512]{3,2,1,0:T(8,128)} %prev_hbm.1, bf16[2,2,1024,512]{3,2,1,0:T(8,128)(2,1)} %rep_hbm.1), custom_call_target="tpu_custom_call" | custom-call | tf_op jit(solution)/shard_map/pallas_call | solution.py:302
  34.1 1.3 %copy.7 = f32[1024]{0:T(1024)} copy(f32[1024]{0:T(1024)} %bitcast.1) | data formatting | bytes 8192
  35.4 1.9 %copy.8 = f32[2,2,64,512]{3,2,1,0:T(8,128)} copy(f32[2,2,64,512]{3,2,1,0:T(8,128)} %get-tuple-element.9) | data formatting | bytes 1048576

commit v2 on v1

v2 whole, which is shorter than its diff:
```python
import functools

import jax
import jax.numpy as jnp
from jax import lax
from jax.experimental import pallas as pl
from jax.experimental.pallas import tpu as pltpu
from jax.sharding import PartitionSpec as P

LINK = jnp.bfloat16
LIFT = 2.0**15.5
MESH = pl.DeviceIdType.MESH


def encode(x):
    x2 = x * x
    x4 = x2 * x2
    x8 = x4 * x4
    return jnp.where(x < 0, -x8, x8).astype(LINK)


def decode(y):
    y = y.astype(jnp.float32)
    root = jnp.exp(0.125 * jnp.log(jnp.maximum(jnp.abs(y), 1e-37)))
    return jnp.where(y < 0, -root, root)


def along(a, b):
    return lax.dot_general(
        a, b, (((1,), (1,)), ((), ())), preferred_element_type=jnp.float32
    )


def dot(a, b):
    return jnp.dot(a, b, preferred_element_type=jnp.float32)


def kernel(
    n, nf, snap_ref, prev_hbm, rep_hbm, power_ref, csdm_ref,
    hbuf, mbuf, prev_ref, rep, columns, weights, diag, lanes, slots,
    osend, zrecv, zsend, srecv, ssend, psend, precv, rsem, vsem,
):
    F, _, S, M = snap_ref.shape
    R = prev_ref.shape[2]
    T = mbuf.shape[1]
    cells = rep.shape[2]
    chips = n // 2
    group = 128
    per = group // R
    me = lax.axis_index("cell")
    fr = lax.axis_index("freq")
    chip, core = me // 2, lax.rem(me, 2)
    sib = chip * 2 + 1 - core

    barrier = pltpu.get_barrier_semaphore()
    for d in (2, n - 2):
        pl.semaphore_signal(barrier, inc=1, device_id=(fr, lax.rem(me + d, n)), device_id_type=MESH)
    pl.semaphore_signal(barrier, inc=1, device_id=(fr, sib), device_id_type=MESH)
    for d in range(1, nf):
        pl.semaphore_signal(barrier, inc=1, device_id=(lax.rem(fr + d, nf), me), device_id_type=MESH)

    earlier = pltpu.make_async_copy(prev_hbm, prev_ref, vsem)
    earlier.start()
    loads = [pltpu.make_async_copy(rep_hbm.at[f], rep.at[f], rsem.at[f]) for f in range(F)]
    for f in range(F):
        loads[f].start()

    def remote(ref, send, recv, to):
        return pltpu.make_async_remote_copy(
            src_ref=ref, dst_ref=ref, send_sem=send, recv_sem=recv,
            device_id=(fr, to), device_id_type=MESH,
        )

    earlier.wait()
    row = lax.broadcasted_iota(jnp.int32, (T, M), 0)
    message = jnp.zeros((T, M), jnp.float32)
    for f in range(F):
        for p in range(2):
            values = snap_ref[f, p].astype(jnp.float32)
            for s in range(S):
                message = jnp.where(row == (f * 2 + p) * S + s, values[s : s + 1, :], message)
        h = prev_ref[f, 0] + prev_ref[f, 1]
        top = jnp.max(jnp.max(jnp.abs(h), axis=1, keepdims=True), axis=0, keepdims=True)
        scale = jnp.maximum(top, 1e-30).astype(jnp.bfloat16).astype(jnp.float32)
        hbuf[me, f] = encode(h * (LIFT / scale))
        message = jnp.where(row == 2 * S * F + f, scale, message)
    mbuf[me] = message.astype(jnp.bfloat16)

    pl.semaphore_wait(barrier, 2 + 1 + nf - 1)

    sends = []
    has_up, has_down = chip + 1 < chips, chip > 0
    up_to, down_to = lax.rem(me + 2, n), lax.rem(me + n - 2, n)
    def piece(x, c):
        return mbuf.at[c] if x == 0 else hbuf.at[c, x - 1]

    for x in range(F + 1):
        own = piece(x, me)

        @pl.when(has_up)
        def _():
            remote(own, osend.at[x, 0], zrecv.at[x, 0, 1], up_to).start()

        @pl.when(has_down)
        def _():
            remote(own, osend.at[x, 1], zrecv.at[x, 1, 1], down_to).start()

        c = remote(own, osend.at[x, 2], srecv.at[x, 1, 0], sib)
        c.start()
        sends.append(c)

    for f in range(F):
        diag[f] = jnp.zeros((1, M), jnp.float32)
        lanes[f] = jnp.zeros((cells, 128), jnp.float32)
    for f in range(F):
        loads[f].wait()

    step = min(512, cells)

    def score(g, f):
        for i in range(per):
            j = g * per + i
            back = mbuf[j].astype(jnp.float32)[2 * S * F + f : 2 * S * F + f + 1, :] * (0.8 / LIFT)
            full = decode(hbuf[j, f]) * back
            ii = lax.broadcasted_iota(jnp.int32, (R, M), 0)
            jj = lax.broadcasted_iota(jnp.int32, (R, M), 1)
            diag[f] += jnp.sum(jnp.where(jj == ii + j * R, full, 0.0), axis=0, keepdims=True)
            top = full.astype(jnp.bfloat16)
            weights[f, i * R : (i + 1) * R] = top
            low = (full - top.astype(jnp.float32)).astype(jnp.bfloat16)
            weights[f, group + i * R : group + (i + 1) * R] = low
        some = pl.ds(pl.multiple_of(g * group, group), group)
        for t in range(cells // step):
            at = slice(t * step, (t + 1) * step)
            us, vs = rep[f, 0, at, some], rep[f, 1, at, some]
            yu = dot(jnp.concatenate([us, us], axis=1), weights[f])
            yv = dot(jnp.concatenate([vs, vs], axis=1), weights[f])
            uf, vf = rep[f, 0, at].astype(jnp.float32), rep[f, 1, at].astype(jnp.float32)
            terms = yu * (uf - vf) + yv * (uf + vf)
            part = terms[:, 0:128]
            for k in range(1, M // 128):
                part = part + terms[:, k * 128 : (k + 1) * 128]
            lanes[f, at] += part

    below, above = chip, chips - 1 - chip
    both = jnp.minimum(below, above)
    longer = jnp.where(below > above, 1, 0)

    def route(i):
        paired = i <= 2 * both
        k = jnp.where(paired, (i + 1) // 2, i - both)
        up = jnp.where(paired, lax.rem(i, 2), longer)
        return 1 - up, k, chip + k * (1 - 2 * up)

    def onward(x, way, k):
        q = chip - k if way == 0 else chip + k
        ref = piece(x, q * 2 + core)
        to = up_to if way == 0 else down_to
        later = jnp.minimum(k + 1, chips - 1)
        return (
            remote(ref, zsend.at[x, way, k], zrecv.at[x, way, k], sib),
            remote(ref, zsend.at[x, way, k], zrecv.at[x, way, later], to),
            remote(ref, ssend.at[x, way, k], srecv.at[x, way, k], sib),
        )

    goes_on = (has_up, has_down)

    def pass_on(k):
        for way in range(2):
            @pl.when((k <= below) if way == 0 else (k <= above))
            def _():
                for x in range(F + 1):
                    arrival, further, across = onward(x, way, k)
                    arrival.wait_recv()

                    @pl.when(goes_on[way])
                    def _():
                        further.start()

                    across.start()

    @pl.loop(0, chips)
    def _(i):
        way, k, q = route(i)
        for x in range(F + 1):
            ref = piece(x, q * 2 + 1 - core)
            remote(ref, ssend.at[x, way, k], srecv.at[x, way, k], sib).wait_recv()
        if 2 * R == group:
            score(q, 0)
        pass_on(i + 1)
        if 2 * R == group:
            for f in range(1, F):
                score(q, f)

    if 2 * R != group:
        @pl.loop(0, M // group)
        def _(g):
            for f in range(F):
                score(g, f)

    factor = 0.2 / (S * n)
    G = mbuf[...].reshape(n * T, M)
    a = lax.broadcasted_iota(jnp.int32, (n * T, n * T), 0)
    b = lax.broadcasted_iota(jnp.int32, (n * T, n * T), 1)
    place = lax.rem(a, T)
    used = place < 2 * S * F
    imag = lax.rem(place, 2 * S) >= S
    turn = jnp.where(used & imag & (b == a - S), 1.0, 0.0) - jnp.where(
        used & jnp.logical_not(imag) & (b == a + S), 1.0, 0.0
    )
    Zf = dot(turn.astype(jnp.bfloat16), G)
    Z = Zf.astype(jnp.bfloat16)
    spot = lax.rem(lax.broadcasted_iota(jnp.int32, (n * T, M), 0), T)
    Gf = G.astype(jnp.float32)
    ready = jnp.zeros((cells, 128), jnp.float32)
    columns[...] = Gf.T
    mine = columns[pl.ds(pl.multiple_of(me * R, R), R), :]
    lane = lax.rem(lax.broadcasted_iota(jnp.int32, (R, n * T), 1), T)
    for f in range(F):
        first, last = 2 * S * f, 2 * S * (f + 1)
        left = jnp.where((lane >= first) & (lane < last), mine, 0.0).astype(jnp.bfloat16)
        csdm_ref[f, 0] = 0.8 * prev_ref[f, 0] + factor * dot(left, G)
        csdm_ref[f, 1] = 0.8 * prev_ref[f, 1] + factor * dot(left, Z)
        inside = (spot >= first) & (spot < last)
        X = jnp.where(inside, Gf, 0.0)
        field = along(rep[f, 0], X.astype(jnp.bfloat16)) - along(
            rep[f, 1], jnp.where(inside, Zf, 0.0).astype(jnp.bfloat16)
        )
        squares = field * field
        part = squares[:, 0:128]
        for k in range(1, n * T // 128):
            part = part + squares[:, k * 128 : (k + 1) * 128]
        every = diag[f] + factor * jnp.sum(X * X, axis=0, keepdims=True)
        gain = (M / (F * nf)) / jnp.sum(every, axis=1, keepdims=True)
        ready = ready + (lanes[f] + factor * part) * gain
    slots[fr] = jnp.sum(ready.T, axis=0, keepdims=True)
    for d in range(1, nf):
        c = pltpu.make_async_remote_copy(
            src_ref=slots.at[fr], dst_ref=slots.at[fr], send_sem=psend.at[d], recv_sem=precv.at[d],
            device_id=(lax.rem(fr + d, nf), me), device_id_type=MESH,
        )
        c.start()
        sends.append(c)

    for x in range(F + 1):
        own = piece(x, me)

        @pl.when(has_up)
        def _():
            remote(own, osend.at[x, 0], zrecv.at[x, 0, 1], up_to).wait_send()

        @pl.when(has_down)
        def _():
            remote(own, osend.at[x, 1], zrecv.at[x, 1, 1], down_to).wait_send()

    @pl.loop(1, chips)
    def _(k):
        for way in range(2):
            @pl.when((k <= below) if way == 0 else (k <= above))
            def _():
                for x in range(F + 1):
                    _, further, across = onward(x, way, k)

                    @pl.when(goes_on[way])
                    def _():
                        further.wait_send()

                    across.wait_send()

    for d in range(1, nf):
        ref = slots.at[lax.rem(fr + nf - d, nf)]
        pltpu.make_async_remote_copy(
            src_ref=ref, dst_ref=ref, send_sem=psend.at[d], recv_sem=precv.at[d],
            device_id=(lax.rem(fr + d, nf), me), device_id_type=MESH,
        ).wait_recv()
    power = slots[0]
    for k in range(1, nf):
        power = power + slots[k]
    power_ref[...] = power
    for c in sends:
        c.wait_send()


def on_device(snapshots, previous, replicas):
    F, _, R, M = previous.shape
    S = snapshots.shape[2]
    cells = replicas.shape[2]
    n, nf = lax.axis_size("cell"), lax.axis_size("freq")
    chips = n // 2
    T = -(-(2 * S * F + F) // 16) * 16
    dma = pltpu.SemaphoreType.DMA
    vmem = pl.BlockSpec(memory_space=pltpu.VMEM)
    hbm = pl.BlockSpec(memory_space=pltpu.HBM)
    power, csdm = pl.pallas_call(
        functools.partial(kernel, n, nf),
        out_shape=(
            jax.ShapeDtypeStruct((1, cells), jnp.float32),
            jax.ShapeDtypeStruct(previous.shape, jnp.float32),
        ),
        in_specs=[vmem, hbm, hbm],
        out_specs=(vmem, vmem),
        scratch_shapes=[
            pltpu.VMEM((n, F, R, M), LINK),
            pltpu.VMEM((n, T, M), jnp.bfloat16),
            pltpu.VMEM(previous.shape, jnp.float32),
            pltpu.VMEM(replicas.shape, jnp.bfloat16),
            pltpu.VMEM((M, n * T), jnp.float32),
            pltpu.VMEM((F, 256, M), jnp.bfloat16),
            pltpu.VMEM((F, 1, M), jnp.float32),
            pltpu.VMEM((F, cells, 128), jnp.float32),
            pltpu.VMEM((nf, 1, cells), jnp.float32),
            dma((F + 1, 3)), dma((F + 1, 2, chips)), dma((F + 1, 2, chips)),
            dma((F + 1, 2, chips)), dma((F + 1, 2, chips)),
            dma((nf,)), dma((nf,)), dma((F,)), dma,
        ],
        compiler_params=pltpu.CompilerParams(
            collective_id=0, has_side_effects=True, vmem_limit_bytes=64 * 1024 * 1024 - 65536
        ),
    )(snapshots, previous, replicas)
    return (power.reshape(cells), csdm)


def solution(mesh):
    placed = (
        P("freq", None, "cell", None),
        P("freq", None, "cell", None),
        P("freq", None, "cell", None),
    )
    return jax.shard_map(
        on_device,
        mesh=mesh,
        in_specs=placed,
        out_specs=(P("cell"), P("freq", None, "cell", None)),
        check_vma=False,
    )
```

time: 37.5 us -> 33.1 us (0.88)
  Pallas kernels: 33.5 us -> 29.1 us
    pallas_call x1, Pallas kernels: 33.5 us -> 29.1 us  [on_device(): pl.pallas_call(functools.partial(kernel, n, nf), out_shape=(jax.ShapeDtyp...]
where the time goes in v2:
time: 33.1 us; the launch traced here: 32.9 us
  Pallas kernels  29.1 us (88%)
  local copies, waits for them, and re-layouts  3.13 us (9%)
  between operations  0.64 us (2%)
    pallas_call x1, Pallas kernels, on_device(): pl.pallas_call(functools.partial(kernel, n, nf), out_shape=(jax.ShapeDtyp...  29.1 us
    unnamed x2, local copies, waits for them, and re-layouts  3.13 us

profile of v2, /device:TPU:0, one launch (start us, length us, event | category | flops | bytes accessed | tf_op | source)
XLA Modules:
  0.0 32.9 jit_solution(12485945001252161418)
XLA Ops:
  0.6 29.1 %shard_map.50 = (f32[1,1024]{1,0:T(1,128)}, f32[2,2,64,512]{3,2,1,0:T(8,128)}) custom-call(bf16[2,2,2,512]{3,2,1,0:T(2,128)(2,1)} %snap_ref.1, f32[2,2,64,512]{3,2,1,0:T(8,128)} %prev_hbm.1, bf16[2,2,1024,512]{3,2,1,0:T(8,128)(2,1)} %rep_hbm.1), custom_call_target="tpu_custom_call" | custom-call | tf_op jit(solution)/shard_map/pallas_call | solution.py:294
  29.7 1.3 %copy.7 = f32[1024]{0:T(1024)} copy(f32[1024]{0:T(1024)} %bitcast.1) | data formatting | bytes 8192
  31.0 1.9 %copy.8 = f32[2,2,64,512]{3,2,1,0:T(8,128)} copy(f32[2,2,64,512]{3,2,1,0:T(8,128)} %get-tuple-element.9) | data formatting | bytes 1048576

commit v3 on v2

--- a/solution.py
+++ b/solution.py
@@ -314,9 +314,9 @@
             dma((nf,)), dma((nf,)), dma((F,)), dma,
         ],
         compiler_params=pltpu.CompilerParams(
-            collective_id=0, has_side_effects=True, vmem_limit_bytes=64 * 1024 * 1024 - 65536
+            collective_id=0, has_side_effects=True, vmem_limit_bytes=48 * 1024 * 1024
         ),
-    )(snapshots, previous, replicas)
+    )(snapshots, pltpu.with_memory_space_constraint(previous, pltpu.HBM), pltpu.with_memory_space_constraint(replicas, pltpu.HBM))
     return (power.reshape(cells), csdm)
 
 

time: 33.1 us -> 30.5 us (0.921)
  Pallas kernels: 29.1 us -> 27.6 us
  local copies, waits for them, and re-layouts: 3.13 us -> 2.08 us
    pallas_call x1, Pallas kernels: 29.1 us -> 27.6 us  [on_device(): pl.pallas_call(functools.partial(kernel, n, nf), out_shape=(jax.ShapeDtyp...]
    unnamed x2 -> x4, local copies, waits for them, and re-layouts: 3.13 us -> 2.08 us
where the time goes in v3:
time: 30.5 us; the launch traced here: 30.3 us
  Pallas kernels  27.6 us (90%)
  local copies, waits for them, and re-layouts  2.08 us (7%)
  between operations  0.65 us (2%)
    pallas_call x1, Pallas kernels, on_device(): pl.pallas_call(functools.partial(kernel, n, nf), out_shape=(jax.ShapeDtyp...  27.6 us
    unnamed x4, local copies, waits for them, and re-layouts  2.08 us

profile of v3, /device:TPU:0, one launch (start us, length us, event | category | flops | bytes accessed | tf_op | source)
XLA Modules:
  0.0 30.3 jit_solution(13898908911414991330)
XLA Ops:
  0.6 0.0 copy-start
  0.6 0.7 %copy-done = bf16[2,2,2,512]{3,2,1,0:T(2,128)(2,1)S(1)} copy-done((bf16[2,2,2,512]{3,2,1,0:T(2,128)(2,1)S(1)}, bf16[2,2,2,512]{3,2,1,0:T(2,128)(2,1)}, u32[]{:S(2)}) %copy-start) | copy-done | bytes 8216
  1.3 27.6 %shard_map.50 = (f32[1,1024]{1,0:T(1,128)S(1)}, f32[2,2,64,512]{3,2,1,0:T(8,128)S(1)}) custom-call(bf16[2,2,2,512]{3,2,1,0:T(2,128)(2,1)S(1)} %copy-done, f32[2,2,64,512]{3,2,1,0:T(8,128)} %prev_hbm.1, bf16[2,2,1024,512]{3,2,1,0:T(8,128)(2,1)} %rep_hbm.1), custom_call_target="tpu_custom_call" | custom-call | tf_op jit(solution)/shard_map/pallas_call | solution.py:294
  28.9 0.6 %copy.7 = f32[1024]{0:T(1024)} copy(f32[1024]{0:T(1024)S(1)} %bitcast.1) | data formatting | bytes 8192
  29.5 0.8 %copy.8 = f32[2,2,64,512]{3,2,1,0:T(8,128)} copy(f32[2,2,64,512]{3,2,1,0:T(8,128)S(1)} %get-tuple-element.9) | data formatting | bytes 1048576
Async XLA Ops:
  0.6 0.7 %copy-start = (bf16[2,2,2,512]{3,2,1,0:T(2,128)(2,1)S(1)}, bf16[2,2,2,512]{3,2,1,0:T(2,128)(2,1)}, u32[]{:S(2)}) copy-start(bf16[2,2,2,512]{3,2,1,0:T(2,128)(2,1)} %snap_ref.1) | copy-start | bytes 24580

commit v4 on v3

--- a/solution.py
+++ b/solution.py
@@ -213,14 +213,8 @@
     spot = lax.rem(lax.broadcasted_iota(jnp.int32, (n * T, M), 0), T)
     Gf = G.astype(jnp.float32)
     ready = jnp.zeros((cells, 128), jnp.float32)
-    columns[...] = Gf.T
-    mine = columns[pl.ds(pl.multiple_of(me * R, R), R), :]
-    lane = lax.rem(lax.broadcasted_iota(jnp.int32, (R, n * T), 1), T)
     for f in range(F):
         first, last = 2 * S * f, 2 * S * (f + 1)
-        left = jnp.where((lane >= first) & (lane < last), mine, 0.0).astype(jnp.bfloat16)
-        csdm_ref[f, 0] = 0.8 * prev_ref[f, 0] + factor * dot(left, G)
-        csdm_ref[f, 1] = 0.8 * prev_ref[f, 1] + factor * dot(left, Z)
         inside = (spot >= first) & (spot < last)
         X = jnp.where(inside, Gf, 0.0)
         field = along(rep[f, 0], X.astype(jnp.bfloat16)) - along(
@@ -241,6 +235,15 @@
         )
         c.start()
         sends.append(c)
+
+    columns[...] = Gf.T
+    mine = columns[pl.ds(pl.multiple_of(me * R, R), R), :]
+    lane = lax.rem(lax.broadcasted_iota(jnp.int32, (R, n * T), 1), T)
+    for f in range(F):
+        first, last = 2 * S * f, 2 * S * (f + 1)
+        left = jnp.where((lane >= first) & (lane < last), mine, 0.0).astype(jnp.bfloat16)
+        csdm_ref[f, 0] = 0.8 * prev_ref[f, 0] + factor * dot(left, G)
+        csdm_ref[f, 1] = 0.8 * prev_ref[f, 1] + factor * dot(left, Z)
 
     for x in range(F + 1):
         own = piece(x, me)

time: 30.5 us -> 30.4 us (level)
  no operation moved by 1% of the time
where the time goes in v4:
time: 30.4 us; the launch traced here: 30.2 us
  Pallas kernels  27.4 us (90%)
  local copies, waits for them, and re-layouts  2.08 us (7%)
  between operations  0.65 us (2%)
    pallas_call x1, Pallas kernels, on_device(): pl.pallas_call(functools.partial(kernel, n, nf), out_shape=(jax.ShapeDtyp...  27.4 us
    unnamed x4, local copies, waits for them, and re-layouts  2.08 us

profile of v4, /device:TPU:0, one launch (start us, length us, event | category | flops | bytes accessed | tf_op | source)
XLA Modules:
  0.0 30.2 jit_solution(6895119515263403969)
XLA Ops:
  0.6 0.0 copy-start
  0.6 0.7 %copy-done = bf16[2,2,2,512]{3,2,1,0:T(2,128)(2,1)S(1)} copy-done((bf16[2,2,2,512]{3,2,1,0:T(2,128)(2,1)S(1)}, bf16[2,2,2,512]{3,2,1,0:T(2,128)(2,1)}, u32[]{:S(2)}) %copy-start) | copy-done | bytes 8216
  1.3 27.4 %shard_map.50 = (f32[1,1024]{1,0:T(1,128)S(1)}, f32[2,2,64,512]{3,2,1,0:T(8,128)S(1)}) custom-call(bf16[2,2,2,512]{3,2,1,0:T(2,128)(2,1)S(1)} %copy-done, f32[2,2,64,512]{3,2,1,0:T(8,128)} %prev_hbm.1, bf16[2,2,1024,512]{3,2,1,0:T(8,128)(2,1)} %rep_hbm.1), custom_call_target="tpu_custom_call" | custom-call | tf_op jit(solution)/shard_map/pallas_call | solution.py:297
  28.8 0.6 %copy.7 = f32[1024]{0:T(1024)} copy(f32[1024]{0:T(1024)S(1)} %bitcast.1) | data formatting | bytes 8192
  29.4 0.8 %copy.8 = f32[2,2,64,512]{3,2,1,0:T(8,128)} copy(f32[2,2,64,512]{3,2,1,0:T(8,128)S(1)} %get-tuple-element.9) | data formatting | bytes 1048576
Async XLA Ops:
  0.6 0.7 %copy-start = (bf16[2,2,2,512]{3,2,1,0:T(2,128)(2,1)S(1)}, bf16[2,2,2,512]{3,2,1,0:T(2,128)(2,1)}, u32[]{:S(2)}) copy-start(bf16[2,2,2,512]{3,2,1,0:T(2,128)(2,1)} %snap_ref.1) | copy-start | bytes 24580
